TPU v7x, 128 devices: a whole 4x4x4 slice. The times are simulated.
128 devices in a mesh: seq: 32 (over z, x, core), ch: 4 (over y).
Axes of the slice: x: 4, y: 4, z: 4, core: 2. Of those that a mesh axis runs over, the one named last changes fastest.
Arguments:
- qkv: bfloat16 [3, 16384, 4096], P(None, 'seq', 'ch'), may hold values from -6 to 6
- short_weight: float32 [3, 3, 4096], P(None, None, 'ch'), may hold values from -3.5 to 3.5
- long_filter: float32 [16384, 4096], P('seq', 'ch'), may hold values from -0.125 to 0.125
- skip: float32 [4096], P('ch'), may hold values from -4 to 4
Outputs:
- mixed: bfloat16 [16384, 4096], P('seq', 'ch')
All inputs are finite; a program needn't handle non-finite values.
Results may differ from a plain program's by a relative error of at most 0.013.
Values may be sent and summed in bfloat16 or wider, within the bound.
A program may use at most 128 MiB of HBM per device.

v0:
```python
import math

import jax
import jax.numpy as jnp
from jax import lax
from jax.sharding import PartitionSpec as P

HIGH = lax.Precision.HIGHEST


def passed_along(value, axis, steps):
    count = lax.axis_size(axis)
    leading, last = (max(0, -steps), min(count, count - steps))
    return lax.ppermute(value, axis, [(source, source + steps) for source in range(leading, last)])


def as_sent(value):

    def short(part):
        return part.astype(jnp.bfloat16) if part.dtype == jnp.float32 else part

    return jax.tree.map(short, value)


def frequency_order(parts):
    place = jnp.arange(parts, dtype=jnp.int32)
    second = jnp.where(place == 0, parts, 2 * parts - place)
    return jnp.stack([place, second], axis=1).reshape(-1)


def along_devices(real_in, order, index, rows, total):
    parts = real_in.shape[0]
    span = 2 * parts
    place = jnp.arange(parts, dtype=jnp.int32)
    angle = 2.0 * math.pi / span * (order[:, None] * place[None, :] % span).astype(jnp.float32)
    cos_mat = jnp.cos(angle)
    sin_mat = jnp.sin(angle)
    real_part = jnp.einsum("ks,sjc->kjc", cos_mat, real_in, precision=HIGH)
    imag_part = -jnp.einsum("ks,sjc->kjc", sin_mat, real_in, precision=HIGH)
    offset = index * rows + jnp.arange(rows, dtype=jnp.int32)
    phase = 2.0 * math.pi / total * (order[:, None] * offset[None, :] % total).astype(jnp.float32)
    cosine = jnp.cos(phase)[:, :, None]
    sine = jnp.sin(phase)[:, :, None]
    return jnp.stack([real_part * cosine + imag_part * sine, imag_part * cosine - real_part * sine])


def token_tables(tok):
    offset = jnp.arange(tok, dtype=jnp.int32)
    angle = 2.0 * math.pi / tok * (offset[:, None] * offset[None, :] % tok).astype(jnp.float32)
    return (jnp.cos(angle), jnp.sin(angle))


def along_tokens(grouped, cos_table, sin_table):
    real_in = grouped[0]
    imag_in = grouped[1]
    real_out = jnp.einsum("kj,pjc->pkc", cos_table, real_in, precision=HIGH) + jnp.einsum(
        "kj,pjc->pkc", sin_table, imag_in, precision=HIGH
    )
    imag_out = jnp.einsum("kj,pjc->pkc", cos_table, imag_in, precision=HIGH) - jnp.einsum(
        "kj,pjc->pkc", sin_table, real_in, precision=HIGH
    )
    return (real_out, imag_out)


def back_tokens(prod_real, prod_imag, cos_table, sin_table, coarse, total):
    tok = prod_real.shape[1]
    real_g = jnp.einsum("jk,pkc->pjc", cos_table, prod_real, precision=HIGH) - jnp.einsum(
        "jk,pkc->pjc", sin_table, prod_imag, precision=HIGH
    )
    imag_g = jnp.einsum("jk,pkc->pjc", cos_table, prod_imag, precision=HIGH) + jnp.einsum(
        "jk,pkc->pjc", sin_table, prod_real, precision=HIGH
    )
    offset = jnp.arange(tok, dtype=jnp.int32)
    phase = 2.0 * math.pi / total * (coarse[:, None] * offset[None, :] % total).astype(jnp.float32)
    cosine = jnp.cos(phase)[:, :, None]
    sine = jnp.sin(phase)[:, :, None]
    return jnp.stack([real_g * cosine - imag_g * sine, imag_g * cosine + real_g * sine])


def back_devices(grouped, order, parts, total):
    span = 2 * parts
    place = jnp.arange(parts, dtype=jnp.int32)
    angle = 2.0 * math.pi / span * (place[:, None] * order[None, :] % span).astype(jnp.float32)
    values = jnp.einsum("sk,kjc->sjc", jnp.cos(angle), grouped[0], precision=HIGH) - jnp.einsum(
        "sk,kjc->sjc", jnp.sin(angle), grouped[1], precision=HIGH
    )
    return values * (1.0 / total)


def on_device(qkv, short_weight, long_filter, skip):
    parts = lax.axis_size("seq")
    index = lax.axis_index("seq")
    tok = qkv.shape[1]
    rows = tok // parts
    span = 2 * parts
    total = span * tok
    order = frequency_order(parts)
    coarse = jnp.stack([index, jnp.where(index == 0, parts, span - index)])
    previous = passed_along(qkv[:, tok - 2 :, :], "seq", 1)
    extended = jnp.concatenate([previous, qkv], axis=1).astype(jnp.float32)
    z = (
        short_weight[:, 0][:, None, :] * extended[:, 2:]
        + short_weight[:, 1][:, None, :] * extended[:, 1:-1]
        + short_weight[:, 2][:, None, :] * extended[:, :-2]
    )
    query = z[0]
    drive = z[1] * z[2]
    cos_table, sin_table = token_tables(tok)
    got_drive, got_kernel = (
        lax.all_to_all(
            drive[None].astype(jnp.bfloat16), "seq", split_axis=1, concat_axis=0, tiled=True
        ).astype(jnp.float32),
        lax.all_to_all(
            long_filter[None].astype(jnp.bfloat16), "seq", split_axis=1, concat_axis=0, tiled=True
        ).astype(jnp.float32),
    )
    part_drive = along_devices(got_drive, order, index, rows, total)
    part_kernel = along_devices(got_kernel, order, index, rows, total)
    group_drive, group_kernel = (
        lax.all_to_all(as_sent(part_drive), "seq", split_axis=1, concat_axis=2, tiled=True).astype(
            part_drive.dtype
        ),
        lax.all_to_all(as_sent(part_kernel), "seq", split_axis=1, concat_axis=2, tiled=True).astype(
            part_kernel.dtype
        ),
    )
    drive_real, drive_imag = along_tokens(group_drive, cos_table, sin_table)
    kernel_real, kernel_imag = along_tokens(group_kernel, cos_table, sin_table)
    prod_real = drive_real * kernel_real - drive_imag * kernel_imag
    prod_imag = drive_real * kernel_imag + drive_imag * kernel_real
    partial_value = back_tokens(prod_real, prod_imag, cos_table, sin_table, coarse, total)
    regathered = lax.all_to_all(
        as_sent(partial_value), "seq", split_axis=2, concat_axis=1, tiled=True
    ).astype(partial_value.dtype)
    values = back_devices(regathered, order, parts, total)
    long_part = lax.all_to_all(
        as_sent(values), "seq", split_axis=0, concat_axis=1, tiled=True
    ).astype(values.dtype)[0]
    return (query * (long_part + skip[None, :] * drive)).astype(jnp.bfloat16)


def solution(mesh):
    return jax.shard_map(
        on_device,
        mesh=mesh,
        in_specs=(P(None, "seq", "ch"), P(None, None, "ch"), P("seq", "ch"), P("ch")),
        out_specs=P("seq", "ch"),
        check_vma=False,
    )
```

profile of v0, /device:TPU:1, one launch (start us, length us, event | category | flops | bytes accessed | tf_op | source)
XLA Modules:
  0.0 423.8 jit_solution(18084500306461204050)
XLA Ops:
  0.8 4.5 %collective-permute-start = (bf16[3,2,1024]{2,1,0:T(2,128)(2,1)S(1)}, bf16[3,2,1024]{2,1,0:T(2,128)(2,1)S(1)}, u32[]{:S(2)}, u32[]{:S(2)}) collective-permute-start(bf16[3,2,1024]{2,1,0:T(2,128)(2,1)S(1)} %slice.55), channel_id=1, source_target_pairs={{0,4},{4,8},{8,12},{12,16},{16,20},{20,24},{24,28},{28,32},{32,36}... | collective-permute-start | bytes 36872 | tf_op jit(solution)/shard_map/ppermute | solution.py:14
  9.3 6.8 %reduce = bf16[512,1024]{1,0:T(8,128)(2,1)S(1)} reduce(bf16[512,1,1024]{2,1,0:T(2,128)(2,1)S(1)} %bitcast.158, bf16[]{:T(256)} %broadcast.321), dimensions={1}, to_apply=%bitcast.139.reduce_sub_computation | reduce | bytes 2097154
  17.7 8.3 %all-to-all-start.2 = ((bf16[32,2,8192]{2,1,0:T(2,128)(2,1)}), bf16[32,2,8192]{2,1,0:T(2,128)(2,1)S(1)}, u32[]{:S(2)}, u32[]{:S(2)}) async-start(bf16[32,2,8192]{2,1,0:T(2,128)(2,1)} %reshape.189), calls=%async_computation.2 | async-start | bytes 2097152 | tf_op jit(solution)/shard_map/all_to_all | solution.py:113
  33.7 7.7 %reduce.1 = bf16[512,1024]{1,0:T(8,128)(2,1)} reduce(bf16[512,1,1024]{2,1,0:T(2,128)(2,1)S(1)} %bitcast.159, bf16[]{:T(256)} %broadcast.321), dimensions={1}, to_apply=%bitcast.140.reduce_sub_computation | reduce | bytes 2097154
  44.0 7.8 %all-to-all-start = ((bf16[32,2,8192]{2,1,0:T(2,128)(2,1)}), bf16[32,2,8192]{2,1,0:T(2,128)(2,1)}, u32[]{:S(2)}, u32[]{:S(2)}) async-start(bf16[32,2,8192]{2,1,0:T(2,128)(2,1)} %reshape.187), calls=%async_computation | async-start | bytes 2097152 | tf_op jit(solution)/shard_map/all_to_all | solution.py:110
  53.4 4.7 %fusion.46 = f32[64,16,1024]{2,0,1:T(8,128)} fusion(bf16[32,16,1024]{2,1,0:T(8,128)(2,1)S(1)} %bitcast.148, s32[64]{0:T(128)S(1)} %mul.391), kind=kOutput, calls=%fused_computation.70 | convolution fusion | flops 402681856 | bytes 5243136 | tf_op jit(solution)/shard_map/ks,sjc->kjc/dot_general | solution.py:39
  58.2 4.7 %fusion.48 = f32[64,16,1024]{2,0,1:T(8,128)} fusion(bf16[32,16,1024]{2,1,0:T(8,128)(2,1)S(1)} %bitcast.149, s32[64]{0:T(128)S(1)} %mul.391), kind=kOutput, calls=%fused_computation.72 | convolution fusion | flops 402681856 | bytes 5243136 | tf_op jit(solution)/shard_map/ks,sjc->kjc/dot_general | solution.py:38
  62.9 6.0 %all-to-all-done = bf16[32,2,8192]{2,1,0:T(2,128)(2,1)} async-done(((bf16[32,2,8192]{2,1,0:T(2,128)(2,1)}), bf16[32,2,8192]{2,1,0:T(2,128)(2,1)}, u32[]{:S(2)}, u32[]{:S(2)}) %all-to-all-start) | async-done | bytes 1048608 | tf_op jit(solution)/shard_map/all_to_all | solution.py:110
  68.9 4.3 %reshape.188 = bf16[512,1,1024]{2,1,0:T(2,128)(2,1)S(1)} reshape(bf16[32,2,8192]{2,1,0:T(2,128)(2,1)} %all-to-all-done) | data formatting | bytes 2097152
  76.7 6.4 %fusion.18 = (bf16[1,64,16,1024]{3,1,2,0:T(8,128)(2,1)S(1)}, bf16[1,64,16,1024]{3,1,2,0:T(8,128)(2,1)S(1)}, bf16[1,64,16,1024]{3,1,2,0:T(8,128)(2,1)S(1)}, bf16[1,64,16,1024]{3,1,2,0:T(8,128)(2,1)}) fusion(f32[64,16,1024]{2,0,1:T(8,128)S(1)} %copy-done.2, f32[64,16,1024]{2,0,1:T(8,128)S(1)} %copy-done.3, f32[64,16]{0,1:T(8,128)S(1)} %get-tuple-element.25, ...), kind=kOutput, calls=%fused_computation.33 | convolution fusion | flops 421556224 | bytes 22028544 | tf_op jit(solution)/shard_map/ks,sjc->kjc/dot_general | solution.py:38
  83.5 4.4 %copy.63 = bf16[2,64,16,1024]{3,2,0,1:T(8,128)(2,1)} copy(bf16[2,64,16,1024]{3,1,2,0:T(8,128)(2,1)S(1)} %pad_maximum_fusion.1) | data formatting | bytes 8388608 | tf_op jit(solution)/shard_map/stack | solution.py:44
  87.9 4.8 %all-to-all-start.3 = ((bf16[2,64,16,1024]{3,2,0,1:T(8,128)(2,1)}), bf16[2,64,16,1024]{3,2,0,1:T(8,128)(2,1)}, u32[]{:S(2)}, u32[]{:S(2)}) async-start(bf16[2,64,16,1024]{3,2,0,1:T(8,128)(2,1)} %copy.63), calls=%async_computation.3 | async-start | bytes 8388608 | tf_op jit(solution)/shard_map/all_to_all | solution.py:123
  94.7 4.4 %copy.54 = bf16[2,64,16,1024]{3,2,0,1:T(8,128)(2,1)} copy(bf16[2,64,16,1024]{3,1,2,0:T(8,128)(2,1)S(1)} %pad_maximum_fusion) | data formatting | bytes 8388608 | tf_op jit(solution)/shard_map/stack | solution.py:44
  99.1 44.0 %all-to-all-done.3 = bf16[2,64,16,1024]{3,2,0,1:T(8,128)(2,1)} async-done(((bf16[2,64,16,1024]{3,2,0,1:T(8,128)(2,1)}), bf16[2,64,16,1024]{3,2,0,1:T(8,128)(2,1)}, u32[]{:S(2)}, u32[]{:S(2)}) %all-to-all-start.3) | async-done | bytes 4194336 | tf_op jit(solution)/shard_map/all_to_all | solution.py:123
  143.1 8.6 %all-to-all-start.1 = ((bf16[2,64,16,1024]{3,2,0,1:T(8,128)(2,1)}), bf16[2,64,16,1024]{3,2,0,1:T(8,128)(2,1)}, u32[]{:S(2)}, u32[]{:S(2)}) async-start(bf16[2,64,16,1024]{3,2,0,1:T(8,128)(2,1)} %copy.54), calls=%async_computation.1 | async-start | bytes 8388608 | tf_op jit(solution)/shard_map/all_to_all | solution.py:120
  155.6 9.9 %fusion.35 = f32[2,1024,512]{2,1,0:T(8,128)S(1)} fusion(bf16[2,512,1024]{2,1,0:T(8,128)(2,1)S(1)} %bitcast.150), kind=kOutput, calls=%fused_computation.58 | convolution fusion | flops 6446120960 | bytes 6291456 | tf_op jit(solution)/shard_map/kj,pjc->pkc/dot_general | solution.py:59
  165.5 9.9 %fusion.39 = f32[2,1024,512]{2,1,0:T(8,128)} fusion(bf16[2,512,1024]{2,1,0:T(8,128)(2,1)S(1)} %bitcast.152), kind=kOutput, calls=%fused_computation.62 | convolution fusion | flops 6446120960 | bytes 6291456 | tf_op jit(solution)/shard_map/kj,pjc->pkc/dot_general | solution.py:56
  175.4 10.4 %convolution_subtract_fusion = f32[2,1024,512]{2,1,0:T(8,128)} fusion(f32[2,1024,512]{2,1,0:T(8,128)S(1)} %fusion.35, bf16[2,512,1024]{2,1,0:T(8,128)(2,1)S(1)} %bitcast.153), kind=kOutput, calls=%fused_computation.25 | convolution fusion | flops 6447169536 | bytes 10485760 | tf_op jit(solution)/shard_map/kj,pjc->pkc/dot_general | solution.py:59
  185.8 16.0 %all-to-all-done.1 = bf16[2,64,16,1024]{3,2,0,1:T(8,128)(2,1)} async-done(((bf16[2,64,16,1024]{3,2,0,1:T(8,128)(2,1)}), bf16[2,64,16,1024]{3,2,0,1:T(8,128)(2,1)}, u32[]{:S(2)}, u32[]{:S(2)}) %all-to-all-start.1) | async-done | bytes 4194336 | tf_op jit(solution)/shard_map/all_to_all | solution.py:120
  205.2 9.9 %fusion.41 = f32[2,1024,512]{2,1,0:T(8,128)S(1)} fusion(bf16[2,512,1024]{2,1,0:T(8,128)(2,1)S(1)} %bitcast.160), kind=kOutput, calls=%fused_computation.64 | convolution fusion | flops 6446120960 | bytes 6291456 | tf_op jit(solution)/shard_map/kj,pjc->pkc/dot_general | solution.py:56
  215.4 10.1 %fusion.37 = f32[2,1024,512]{2,1,0:T(8,128)} fusion(bf16[2,512,1024]{2,1,0:T(8,128)(2,1)S(1)} %bitcast.154), kind=kOutput, calls=%fused_computation.60 | convolution fusion | flops 6446120960 | bytes 6291456 | tf_op jit(solution)/shard_map/kj,pjc->pkc/dot_general | solution.py:59
  225.5 9.8 %convolution_add_fusion.1 = f32[2,1024,512]{2,1,0:T(8,128)S(1)} fusion(f32[2,1024,512]{2,1,0:T(8,128)S(1)} %fusion.41, bf16[2,512,1024]{2,1,0:T(8,128)(2,1)S(1)} %bitcast.155), kind=kOutput, calls=%fused_computation.28 | convolution fusion | flops 6447169536 | bytes 10485760 | tf_op jit(solution)/shard_map/kj,pjc->pkc/dot_general | solution.py:56
  235.3 10.2 %convolution_add_fusion = f32[2,1024,512]{2,1,0:T(8,128)S(1)} fusion(f32[2,1024,512]{2,1,0:T(8,128)S(1)} %copy-done.6, bf16[2,512,1024]{2,1,0:T(8,128)(2,1)S(1)} %bitcast.151), kind=kOutput, calls=%fused_computation.27 | convolution fusion | flops 6447169536 | bytes 10485760 | tf_op jit(solution)/shard_map/kj,pjc->pkc/dot_general | solution.py:56
  245.5 13.0 %multiply_subtract_fusion = (f32[2,1024,512]{2,1,0:T(8,128)S(1)}, f32[2,1024,512]{2,1,0:T(8,128)S(1)}) fusion(f32[2,1024,512]{2,1,0:T(8,128)S(1)} %copy-done.1, f32[2,1024,512]{2,1,0:T(8,128)S(1)} %convolution_add_fusion.1, f32[2,1024,512]{2,1,0:T(8,128)S(1)} %convolution_add_fusion, f32[2,1024,512]{2,1,0:T(8,128)} %fusion.37, ...), kind=kOutput, calls=%fused_computation.19 | convolution fusion | flops 6453460992 | bytes 27262976 | tf_op jit(solution)/shard_map/kj,pjc->pkc/dot_general | solution.py:59
  258.5 10.7 %fusion.4 = f32[2,1024,512]{2,1,0:T(8,128)S(1)} fusion(f32[2,1024,512]{2,1,0:T(8,128)S(1)} %get-tuple-element.6), kind=kOutput, calls=%fused_computation.10 | convolution fusion | flops 6446120960 | bytes 8388608 | tf_op jit(solution)/shard_map/jk,pkc->pjc/dot_general | solution.py:67
  269.2 11.5 %fusion.2 = f32[2,1024,512]{2,1,0:T(8,128)S(1)} fusion(f32[2,1024,512]{2,1,0:T(8,128)S(1)} %get-tuple-element.6), kind=kOutput, calls=%fused_computation.8 | convolution fusion | flops 6446120960 | bytes 8388608 | tf_op jit(solution)/shard_map/jk,pkc->pjc/dot_general | solution.py:70
  280.7 11.5 %fusion.10 = f32[2,1024,512]{2,1,0:T(8,128)S(1)} fusion(f32[2,1024,512]{2,1,0:T(8,128)S(1)} %fusion.4, f32[2,1024,512]{2,1,0:T(8,128)S(1)} %get-tuple-element.5), kind=kOutput, calls=%fused_computation.29 | convolution fusion | flops 6447169536 | bytes 12582912 | tf_op jit(solution)/shard_map/jk,pkc->pjc/dot_general | solution.py:67
  292.2 11.6 %fusion.20 = (bf16[1,2,512,1024]{2,3,1,0:T(8,128)(2,1)S(1)}, bf16[1,2,512,1024]{2,3,1,0:T(8,128)(2,1)S(1)}) fusion(f32[2,1024,512]{2,1,0:T(8,128)S(1)} %fusion.10, f32[2,512]{1,0:T(2,128)S(1)} %get-tuple-element.27, f32[2,512]{1,0:T(2,128)S(1)} %get-tuple-element.26, f32[2,1024,512]{2,1,0:T(8,128)S(1)} %fusion.2, f32[2,1024,512]{2,1,0:T(8,128)S(1)} %get-tuple-element.5), kind=kOutput, calls=%fused_computation.35 | convolution fusion | flops 6455558144 | bytes 16785408 | tf_op jit(solution)/shard_map/jk,pkc->pjc/dot_general | solution.py:70
  306.2 11.4 %copy.73 = bf16[2,2,512,1024]{3,1,0,2:T(2,128)(2,1)} copy(bf16[2,2,512,1024]{2,3,1,0:T(8,128)(2,1)} %pad_maximum_fusion.2) | data formatting | bytes 8388608 | tf_op jit(solution)/shard_map/stack | solution.py:77
  317.6 58.5 %all_to_all.78 = bf16[2,2,512,1024]{3,1,0,2:T(2,128)(2,1)S(1)} all-to-all(bf16[2,2,512,1024]{3,1,0,2:T(2,128)(2,1)} %copy.73), channel_id=1, replica_groups=mesh['seq'=32,'ch'=4] {'seq'}, dimensions={2} | all-to-all | bytes 8388608 | tf_op jit(solution)/shard_map/all_to_all | solution.py:132
  391.7 4.4 %squeeze.30 = bf16[64,16,1024]{2,0,1:T(8,128)(2,1)} reshape(bf16[1,32,2,16,1024]{4,2,1,3,0:T(2,128)(2,1)} %copy.76) | data formatting | bytes 4194304 | tf_op jit(solution)/shard_map/squeeze | solution.py:85
  400.1 21.4 %all_to_all.79 = bf16[32,16,1024]{2,1,0:T(8,128)(2,1)S(1)} all-to-all(bf16[32,16,1024]{2,1,0:T(8,128)(2,1)S(1)} %copy.77), channel_id=1, replica_groups=mesh['seq'=32,'ch'=4] {'seq'}, dimensions={0} | all-to-all | bytes 2097152 | tf_op jit(solution)/shard_map/all_to_all | solution.py:136
  (71 shorter events, 55.3 us)
Async XLA Ops:
  0.8 25.5 %collective-permute-start = (bf16[3,2,1024]{2,1,0:T(2,128)(2,1)S(1)}, bf16[3,2,1024]{2,1,0:T(2,128)(2,1)S(1)}, u32[]{:S(2)}, u32[]{:S(2)}) collective-permute-start(bf16[3,2,1024]{2,1,0:T(2,128)(2,1)S(1)} %slice.55), channel_id=1, source_target_pairs={{0,4},{4,8},{8,12},{12,16},{16,20},{20,24},{24,28},{28,32},{32,36}... | collective-permute-start | bytes 36872 | tf_op jit(solution)/shard_map/ppermute | solution.py:14
  8.7 17.3 %copy-start.7 = (f32[3,3,1024]{2,1,0:T(4,128)S(1)}, f32[3,3,1024]{2,1,0:T(4,128)}, u32[]{:S(2)}) copy-start(f32[3,3,1024]{2,1,0:T(4,128)} %param.5) | copy-start | bytes 110596
  17.7 26.4 %all-to-all-start.2 = ((bf16[32,2,8192]{2,1,0:T(2,128)(2,1)}), bf16[32,2,8192]{2,1,0:T(2,128)(2,1)S(1)}, u32[]{:S(2)}, u32[]{:S(2)}) async-start(bf16[32,2,8192]{2,1,0:T(2,128)(2,1)} %reshape.189), calls=%async_computation.2 | async-start | bytes 2097152 | tf_op jit(solution)/shard_map/all_to_all | solution.py:113
  31.0 2.7 copy-start
  44.0 24.9 %all-to-all-start = ((bf16[32,2,8192]{2,1,0:T(2,128)(2,1)}), bf16[32,2,8192]{2,1,0:T(2,128)(2,1)}, u32[]{:S(2)}, u32[]{:S(2)}) async-start(bf16[32,2,8192]{2,1,0:T(2,128)(2,1)} %reshape.187), calls=%async_computation | async-start | bytes 2097152 | tf_op jit(solution)/shard_map/all_to_all | solution.py:110
  73.2 3.1 copy-start.2
  73.2 3.5 copy-start.3
  87.9 55.2 %all-to-all-start.3 = ((bf16[2,64,16,1024]{3,2,0,1:T(8,128)(2,1)}), bf16[2,64,16,1024]{3,2,0,1:T(8,128)(2,1)}, u32[]{:S(2)}, u32[]{:S(2)}) async-start(bf16[2,64,16,1024]{3,2,0,1:T(8,128)(2,1)} %copy.63), calls=%async_computation.3 | async-start | bytes 8388608 | tf_op jit(solution)/shard_map/all_to_all | solution.py:123
  143.1 58.7 %all-to-all-start.1 = ((bf16[2,64,16,1024]{3,2,0,1:T(8,128)(2,1)}), bf16[2,64,16,1024]{3,2,0,1:T(8,128)(2,1)}, u32[]{:S(2)}, u32[]{:S(2)}) async-start(bf16[2,64,16,1024]{3,2,0,1:T(8,128)(2,1)} %copy.54), calls=%async_computation.1 | async-start | bytes 8388608 | tf_op jit(solution)/shard_map/all_to_all | solution.py:120
  205.1 10.2 %copy-start.5 = (bf16[1,2,32,16,1024]{4,3,2,1,0:T(8,128)(2,1)}, bf16[1,2,32,16,1024]{4,3,2,1,0:T(8,128)(2,1)S(1)}, u32[]{:S(2)}) copy-start(bf16[1,2,32,16,1024]{4,3,2,1,0:T(8,128)(2,1)S(1)} %copy.56) | copy-start | bytes 6291460
  225.5 9.8 %copy-start.6 = (f32[2,1024,512]{2,1,0:T(8,128)S(1)}, f32[2,1024,512]{2,1,0:T(8,128)}, u32[]{:S(2)}) copy-start(f32[2,1024,512]{2,1,0:T(8,128)} %fusion.39) | copy-start | bytes 12582916
  235.3 10.2 %copy-start.1 = (f32[2,1024,512]{2,1,0:T(8,128)S(1)}, f32[2,1024,512]{2,1,0:T(8,128)}, u32[]{:S(2)}) copy-start(f32[2,1024,512]{2,1,0:T(8,128)} %convolution_subtract_fusion) | copy-start | bytes 12582916
  384.0 4.2 copy-start.4
  391.7 29.8 %slice-start = ((s8[6291456]{0:T(1024)(128)(4,1)}), s8[2097152]{0:T(1024)(128)(4,1)S(1)}, s32[]{:S(2)}) async-start(s8[6291456]{0:T(1024)(128)(4,1)} %bitcast.141), calls=%async_computation.6 | async-start | bytes 4194304
  396.0 25.5 %slice-start.1 = ((s8[6291456]{0:T(1024)(128)(4,1)}), s8[4194304]{0:T(1024)(128)(4,1)S(1)}, s32[]{:S(2)}) async-start(s8[6291456]{0:T(1024)(128)(4,1)} %bitcast.141), calls=%async_computation.7 | async-start | bytes 8388608
  396.0 25.5 %copy-start.8 = (f32[1024]{0:T(1024)S(1)}, f32[1024]{0:T(1024)}, u32[]{:S(2)}) copy-start(f32[1024]{0:T(1024)} %param.7) | copy-start | bytes 12292
where the time goes:
time: 432 us; the launch traced here: 424 us
  matrix products  155 us (36%)
  blocking collectives  79.9 us (18%)
  waiting for transfers between devices  66 us (15%)
  local copies, waits for them, and re-layouts  60 us (14%)
  starting transfers between devices  34 us (8%)
  other arithmetic  28.3 us (7%)
    all_to_all x1, blocking collectives, on_device(): lax.all_to_all(as_sent(partial_value), 'seq', split_axis=2, concat_axis=1...  58.5 us
    all_to_all x1, waiting for transfers between devices, on_device(): lax.all_to_all(as_sent(part_kernel), 'seq', split_axis=1, concat_axis=2,...  44 us
    dot_general x2, matrix products, along_tokens(): jnp.einsum('kj,pjc->pkc', sin_table, real_in, precision=HIGH)  23.5 us
    all_to_all x1, blocking collectives, on_device(): lax.all_to_all(as_sent(values), 'seq', split_axis=0, concat_axis=1, tiled...  21.4 us
    dot_general x2, matrix products, along_tokens(): jnp.einsum('kj,pjc->pkc', cos_table, imag_in, precision=HIGH)  20 us
    dot_general x2, matrix products, along_tokens(): jnp.einsum('kj,pjc->pkc', sin_table, imag_in, precision=HIGH)  19.9 us
    dot_general x2, matrix products, along_tokens(): jnp.einsum('kj,pjc->pkc', cos_table, real_in, precision=HIGH)  19.8 us
    all_to_all x1, waiting for transfers between devices, on_device(): lax.all_to_all(as_sent(part_drive), 'seq', split_axis=1, concat_axis=2, t...  16 us
  transfers between devices with their start and end apart: 5, of which 3 were waited for; matrix products, arithmetic and copies ran while one was open for 19% of the time, Pallas kernels for 0%

commit v1 on v0

v1 whole, which is shorter than its diff:
```python
import functools

import jax
import jax.numpy as jnp
import numpy as np
from jax import lax
from jax.experimental import pallas as pl
from jax.experimental.pallas import tpu as pltpu
from jax.sharding import PartitionSpec as P

MESH = pl.DeviceIdType.MESH
R = 16
F32 = jnp.float32
BF16 = jnp.bfloat16


def dot(a, b):
    return jnp.dot(a, b, preferred_element_type=F32)


def tables(parts, tok):
    place = np.arange(parts)
    odd = 2 * place + 1
    angle = 2 * np.pi * np.outer(odd, place) / (4 * parts)
    spread = lambda m: np.kron(m, np.eye(R))
    f1 = np.concatenate([spread(np.cos(angle)), spread(-np.sin(angle))], axis=0)
    g1 = np.concatenate([spread(np.cos(angle).T), spread(-np.sin(angle).T)], axis=1)
    offset = np.arange(tok)
    angle = 2 * np.pi * (np.outer(offset, offset) % tok) / tok
    cos, sin = np.cos(angle), np.sin(angle)
    w = np.block([[cos, -sin], [sin, cos]])
    wi = np.block([[cos, sin], [-sin, cos]])
    angle = 2 * np.pi * np.outer(odd, offset) / (4 * parts * tok)
    tw = np.stack([np.cos(angle), np.sin(angle)])
    half = lambda m: jnp.asarray(m.astype(np.float32), BF16)
    return half(f1), half(w), half(wi), half(g1), jnp.asarray(tw.astype(np.float32))


def kernel(
    parts, qkv_hbm, sw_ref, filt_hbm, skip_ref, f1_hbm, w_hbm, wi_hbm, g1_hbm, tw_ref, o_ref,
    qkv, filt, f1, w, wi, g1, halo, ht, dt, hr, xr, ys, lt, drive, query, spec, b, y, g,
    load_sem, halo_sem, send_sem, recv_sem,
):
    me = lax.axis_index("seq")
    ch = lax.axis_index("ch")
    tok = qkv.shape[1]
    chans = qkv.shape[2]
    rows = parts * R
    chunks = chans // rows
    half = tok // 2

    barrier = pltpu.get_barrier_semaphore()

    def greet(k, carry):
        pl.semaphore_signal(barrier, inc=1, device_id=(lax.rem(me + k, parts), ch), device_id_type=MESH)
        return carry

    lax.fori_loop(1, parts, greet, 0)

    loads = [
        pltpu.make_async_copy(src, dst, load_sem.at[i])
        for i, (src, dst) in enumerate(
            [(filt_hbm, filt), (qkv_hbm, qkv), (f1_hbm, f1), (w_hbm, w), (wi_hbm, wi), (g1_hbm, g1)]
        )
    ]
    for load in loads:
        load.start()

    loads[0].wait()

    def turn_filter(j, carry):
        at = pl.ds(pl.multiple_of(j * 128, 128), 128)
        ht[at, :] = filt[:, at].T.astype(BF16)
        return carry

    lax.fori_loop(0, chans // 128, turn_filter, 0)
    loads[1].wait()
    pl.semaphore_wait(barrier, parts - 1)

    edge = pltpu.make_async_remote_copy(
        src_ref=qkv.at[:, pl.ds(tok - 16, 16), :], dst_ref=halo, send_sem=halo_sem.at[0], recv_sem=halo_sem.at[1],
        device_id=(lax.rem(me + 1, parts), ch), device_id_type=MESH,
    )
    edge.start()

    def deal(kind, chunk, src, dst):
        base = chunk * rows

        def one(k, carry):
            to = lax.rem(me + k, parts)
            pltpu.make_async_remote_copy(
                src_ref=src.at[pl.ds(pl.multiple_of(base + to * R, R), R), :],
                dst_ref=dst.at[pl.ds(pl.multiple_of(base + me * R, R), R), :],
                send_sem=send_sem.at[kind, chunk],
                recv_sem=recv_sem.at[kind, chunk],
                device_id=(to, ch),
                device_id_type=MESH,
            ).start()
            return carry

        lax.fori_loop(1, parts, one, 0)
        own = pl.ds(pl.multiple_of(base + me * R, R), R)
        pltpu.make_async_copy(src.at[own, :], dst.at[own, :], recv_sem.at[kind, chunk]).start()

    def arrived(kind, chunk, dst):
        whole = dst.at[pl.ds(chunk * rows, rows), :]
        pltpu.make_async_copy(whole, whole, recv_sem.at[kind, chunk]).wait()

    def left(kind, chunk, src):
        sent = src.at[pl.ds(0, rows - R), :]
        pltpu.make_async_copy(sent, sent, send_sem.at[kind, chunk]).wait()

    for chunk in range(chunks):
        deal(0, chunk, ht, hr)

    edge.wait_recv()
    first = jnp.where(me > 0, 1.0, 0.0).astype(F32)

    def short(m, at):
        before = halo[m, :, at].astype(F32)[8:, :] * first
        ext = jnp.concatenate([before, qkv[m, :, at].astype(F32)], axis=0)
        return (
            sw_ref[m, 0:1, at] * ext[8:, :]
            + sw_ref[m, 1:2, at] * ext[7:-1, :]
            + sw_ref[m, 2:3, at] * ext[6:-2, :]
        )

    for chunk in range(chunks):

        def gate(j, carry):
            at = pl.ds(pl.multiple_of(chunk * rows + j * 128, 128), 128)
            value = short(1, at) * short(2, at)
            drive[:, at] = value
            dt[at, :] = value.T.astype(BF16)
            return carry

        lax.fori_loop(0, rows // 128, gate, 0)
        deal(1, chunk, dt, xr)

    def ask(j, carry):
        at = pl.ds(pl.multiple_of(j * 128, 128), 128)
        query[:, at] = short(0, at)
        return carry

    lax.fori_loop(0, chans // 128, ask, 0)

    def along_parts(blocks, chunk):
        for j in range(2):
            real = dot(f1[j * rows // 2 : (j + 1) * rows // 2, :], blocks)
            imag = dot(f1[rows + j * rows // 2 : rows + (j + 1) * rows // 2, :], blocks)
            for k in range(parts // 2):
                at = j * (parts // 2) + k
                cos, sin = tw_ref[0, at : at + 1, :], tw_ref[1, at : at + 1, :]
                re, im = real[k * R : (k + 1) * R, :], imag[k * R : (k + 1) * R, :]
                b[at * R : (at + 1) * R, :tok] = (re * cos + im * sin).astype(BF16)
                b[at * R : (at + 1) * R, tok:] = (im * cos - re * sin).astype(BF16)

    for load in loads[2:]:
        load.wait()

    for chunk in range(chunks):
        arrived(0, chunk, hr)
        along_parts(hr[pl.ds(chunk * rows, rows), :], chunk)
        for n in range(4):
            spec[chunk, :, n * half : (n + 1) * half] = dot(b[...], w[:, n * half : (n + 1) * half])

    for chunk in range(chunks):
        arrived(1, chunk, xr)
        along_parts(xr[pl.ds(chunk * rows, rows), :], chunk)
        for n in range(2):
            real_at, imag_at = slice(n * half, (n + 1) * half), slice(tok + n * half, tok + (n + 1) * half)
            xre, xim = dot(b[...], w[:, real_at]), dot(b[...], w[:, imag_at])
            hre, him = spec[chunk, :, real_at], spec[chunk, :, imag_at]
            y[:, real_at] = (xre * hre - xim * him).astype(BF16)
            y[:, imag_at] = (xre * him + xim * hre).astype(BF16)
        for n in range(2):
            real_at, imag_at = slice(n * half, (n + 1) * half), slice(tok + n * half, tok + (n + 1) * half)
            gre, gim = dot(y[...], wi[:, real_at]), dot(y[...], wi[:, imag_at])
            for k in range(parts):
                scale = 2.0 / (2 * parts * tok)
                cos, sin = tw_ref[0, k : k + 1, real_at] * scale, tw_ref[1, k : k + 1, real_at] * scale
                re, im = gre[k * R : (k + 1) * R, :], gim[k * R : (k + 1) * R, :]
                g[k * R : (k + 1) * R, real_at] = (re * cos - im * sin).astype(BF16)
                g[rows + k * R : rows + (k + 1) * R, real_at] = (im * cos + re * sin).astype(BF16)
        for n in range(2):
            at = slice(n * half, (n + 1) * half)
            ys[pl.ds(chunk * rows, rows), at] = dot(g1[...], g[:, at]).astype(BF16)
        deal(2, chunk, ys, lt)

    for chunk in range(chunks):
        arrived(2, chunk, lt)

        def finish(j, carry):
            at = pl.ds(pl.multiple_of(chunk * rows + j * 128, 128), 128)
            long_part = lt[at, :].astype(F32).T
            o_ref[:, at] = (query[:, at] * (long_part + skip_ref[0:1, at] * drive[:, at])).astype(BF16)
            return carry

        lax.fori_loop(0, rows // 128, finish, 0)

    edge.wait_send()
    for chunk in range(chunks):
        left(0, chunk, ht)
        left(1, chunk, dt)
        left(2, chunk, ys)


def solution(mesh):
    parts = mesh.shape["seq"]

    def on_device(qkv, short_weight, long_filter, skip):
        tok, chans = long_filter.shape
        rows = parts * R
        chunks = chans // rows
        f1, w, wi, g1, tw = tables(parts, tok)
        vmem = pl.BlockSpec(memory_space=pltpu.VMEM)
        hbm = pl.BlockSpec(memory_space=pl.ANY)
        return pl.pallas_call(
            functools.partial(kernel, parts),
            out_shape=jax.ShapeDtypeStruct((tok, chans), BF16),
            in_specs=[hbm, vmem, hbm, vmem, hbm, hbm, hbm, hbm, vmem],
            out_specs=vmem,
            scratch_shapes=[
                pltpu.VMEM(qkv.shape, BF16),
                pltpu.VMEM((tok, chans), F32),
                pltpu.VMEM(f1.shape, BF16),
                pltpu.VMEM(w.shape, BF16),
                pltpu.VMEM(wi.shape, BF16),
                pltpu.VMEM(g1.shape, BF16),
                pltpu.VMEM((3, 16, chans), BF16),
                pltpu.VMEM((chans, tok), BF16),
                pltpu.VMEM((chans, tok), BF16),
                pltpu.VMEM((chans, tok), BF16),
                pltpu.VMEM((chans, tok), BF16),
                pltpu.VMEM((chans, tok), BF16),
                pltpu.VMEM((chans, tok), BF16),
                pltpu.VMEM((tok, chans), F32),
                pltpu.VMEM((tok, chans), F32),
                pltpu.VMEM((chunks, rows, 2 * tok), F32),
                pltpu.VMEM((rows, 2 * tok), BF16),
                pltpu.VMEM((rows, 2 * tok), BF16),
                pltpu.VMEM((2 * rows, tok), BF16),
                pltpu.SemaphoreType.DMA((6,)),
                pltpu.SemaphoreType.DMA((2,)),
                pltpu.SemaphoreType.DMA((3, chunks)),
                pltpu.SemaphoreType.DMA((3, chunks)),
            ],
            compiler_params=pltpu.CompilerParams(
                collective_id=0, has_side_effects=True, vmem_limit_bytes=60 * 2**20
            ),
        )(qkv, short_weight, long_filter, skip[None, :], f1, w, wi, g1, tw)

    return jax.shard_map(
        on_device,
        mesh=mesh,
        in_specs=(P(None, "seq", "ch"), P(None, None, "ch"), P("seq", "ch"), P("ch")),
        out_specs=P("seq", "ch"),
        check_vma=False,
    )
```

time: 432 us -> 52.9 us (0.12); the launches traced: 424 us -> 52.2 us
  matrix products: 155 us -> 0 us
  blocking collectives: 79.9 us -> 0 us
  waiting for transfers between devices: 66 us -> 0 us
  local copies, waits for them, and re-layouts: 60 us -> 2.26 us
  Pallas kernels: 0 us -> 49.9 us
  starting transfers between devices: 34 us -> 0 us
  other arithmetic: 28.3 us -> 0 us
    dot_general x18 -> x0, matrix products: 155 us -> none  [the longest x2 23.5 us: along_tokens(): jnp.einsum('kj,pjc->pkc', sin_table, real_in, precision=HIGH)]
    all_to_all x2 -> x0, blocking collectives: 79.9 us -> none  [the longest x1 58.5 us: on_device(): lax.all_to_all(as_sent(partial_value), 'seq', split_axis=2, concat_axis=1...]
    all_to_all x4 -> x0, waiting for transfers between devices: 66 us -> none  [the longest x1 44 us: on_device(): lax.all_to_all(as_sent(part_kernel), 'seq', split_axis=1, concat_axis=2,...]
    pallas_call x0 -> x1, Pallas kernels: none -> 49.9 us  [on_device(): pl.pallas_call(functools.partial(kernel, parts), out_shape=jax.ShapeDtype...]
    all_to_all x4 -> x0, starting transfers between devices: 29.5 us -> none  [the longest x1 8.56 us: on_device(): lax.all_to_all(as_sent(part_drive), 'seq', split_axis=1, concat_axis=2, t...]
    another operation x4 -> x0, local copies, waits for them, and re-layouts: 20.3 us -> none  [the longest x1 11.4 us: back_tokens(): jnp.stack([real_g * cosine - imag_g * sine, imag_g * cosine + real_g * si...]
    unnamed x3 -> x0, other arithmetic: 14.5 us -> none
    slice x11 -> x0, local copies, waits for them, and re-layouts: 10.5 us -> none  [the longest x2 5.52 us: back_devices(): grouped[1]]
  transfers between devices with their start and end apart: 5 -> 0, of which waited for: 3 -> 0; matrix products, arithmetic and copies ran while one was open for 19% -> 0% of each run, Pallas kernels for 0% -> 0%
where the time goes in v1:
time: 52.9 us; the launch traced here: 52.2 us
  Pallas kernels  49.9 us (94%)
  local copies, waits for them, and re-layouts  2.26 us (4%)
    pallas_call x1, Pallas kernels, on_device(): pl.pallas_call(functools.partial(kernel, parts), out_shape=jax.ShapeDtype...  49.9 us
    unnamed x1, local copies, waits for them, and re-layouts  2.26 us

profile of v1, /device:TPU:1, one launch (start us, length us, event | category | flops | bytes accessed | tf_op | source)
XLA Modules:
  0.0 52.2 jit_solution(754675722514011762)
XLA Ops:
  0.0 49.9 %shard_map.91 = bf16[512,1024]{1,0:T(8,128)(2,1)} custom-call(bf16[3,512,1024]{2,1,0:T(8,128)(2,1)} %qkv_hbm.1, f32[3,3,1024]{2,1,0:T(4,128)} %sw_ref.1, f32[512,1024]{1,0:T(8,128)} %filt_hbm.1, f32[1,1024]{1,0:T(1,128)} %bitcast.1, bf16[1024,512]{1,0:T(8,128)(2,1)} %constant.10.clone.f1_hbm, bf16[1024,1024]{1,0:T(8,128)(2,1)} %constant.11.clone.w_hbm, ...), custom_call_target="tpu_custom_call" | custom-call | tf_op jit(solution)/shard_map/pallas_call | solution.py:218
  49.9 2.3 %copy.11 = bf16[512,1024]{1,0:T(8,128)(2,1)} copy(bf16[512,1024]{1,0:T(8,128)(2,1)} %shard_map.91) | data formatting | bytes 2097152

commit v2 on v1

--- a/solution.py
+++ b/solution.py
@@ -10,6 +10,7 @@
 
 MESH = pl.DeviceIdType.MESH
 R = 16
+STEPS = ((2, 2), (2, 1), (1, 2), (2, 3), (3, 2), (1, 1), (3, 3), (1, 3), (3, 1), (2, 0), (0, 2), (0, 1), (1, 0), (0, 3), (3, 0))
 F32 = jnp.float32
 BF16 = jnp.bfloat16
 
@@ -38,7 +39,7 @@
 
 def kernel(
     parts, qkv_hbm, sw_ref, filt_hbm, skip_ref, f1_hbm, w_hbm, wi_hbm, g1_hbm, tw_ref, o_ref,
-    qkv, filt, f1, w, wi, g1, halo, ht, dt, hr, xr, ys, lt, drive, query, spec, b, y, g,
+    qkv, filt, f1, w, wi, g1, tail, ends, halo, ht, dt, hr, xr, ys, lt, drive, query, spec, b, y, g,
     load_sem, halo_sem, send_sem, recv_sem,
 ):
     me = lax.axis_index("seq")
@@ -49,45 +50,48 @@
     chunks = chans // rows
     half = tok // 2
 
-    barrier = pltpu.get_barrier_semaphore()
-
-    def greet(k, carry):
-        pl.semaphore_signal(barrier, inc=1, device_id=(lax.rem(me + k, parts), ch), device_id_type=MESH)
-        return carry
-
-    lax.fori_loop(1, parts, greet, 0)
-
+    lanes = [pl.ds(chunk * rows, rows) for chunk in range(chunks)]
     loads = [
         pltpu.make_async_copy(src, dst, load_sem.at[i])
         for i, (src, dst) in enumerate(
-            [(filt_hbm, filt), (qkv_hbm, qkv), (f1_hbm, f1), (w_hbm, w), (wi_hbm, wi), (g1_hbm, g1)]
+            [(filt_hbm.at[:, at], filt.at[:, at]) for at in lanes]
+            + [(qkv_hbm.at[:, pl.ds(tok - 16, 16), :], tail)]
+            + [(qkv_hbm, qkv), (f1_hbm, f1), (w_hbm, w), (wi_hbm, wi), (g1_hbm, g1)]
         )
     ]
-    for load in loads:
+    for load in loads[: chunks + 1]:
         load.start()
 
-    loads[0].wait()
+    barrier = pltpu.get_barrier_semaphore()
+
+    def greet(k, carry):
+        pl.semaphore_signal(barrier, inc=1, device_id=((me + k) & (parts - 1), ch), device_id_type=MESH)
+        return carry
+
+    lax.fori_loop(1, parts, greet, 0)
 
     def turn_filter(j, carry):
         at = pl.ds(pl.multiple_of(j * 128, 128), 128)
         ht[at, :] = filt[:, at].T.astype(BF16)
         return carry
 
-    lax.fori_loop(0, chans // 128, turn_filter, 0)
-    loads[1].wait()
+    loads[0].wait()
+    lax.fori_loop(0, rows // 128, turn_filter, 0)
+    loads[chunks].wait()
+    last = [tail[m].astype(F32)[14:, :] for m in range(3)]
+    ends[...] = jnp.concatenate(last + [jnp.zeros((10, chans), F32)], axis=0).astype(BF16)
     pl.semaphore_wait(barrier, parts - 1)
 
     edge = pltpu.make_async_remote_copy(
-        src_ref=qkv.at[:, pl.ds(tok - 16, 16), :], dst_ref=halo, send_sem=halo_sem.at[0], recv_sem=halo_sem.at[1],
-        device_id=(lax.rem(me + 1, parts), ch), device_id_type=MESH,
+        src_ref=ends, dst_ref=halo, send_sem=halo_sem.at[0], recv_sem=halo_sem.at[1],
+        device_id=((me + 1) & (parts - 1), ch), device_id_type=MESH,
     )
     edge.start()
 
     def deal(kind, chunk, src, dst):
         base = chunk * rows
 
-        def one(k, carry):
-            to = lax.rem(me + k, parts)
+        def send(to):
             pltpu.make_async_remote_copy(
                 src_ref=src.at[pl.ds(pl.multiple_of(base + to * R, R), R), :],
                 dst_ref=dst.at[pl.ds(pl.multiple_of(base + me * R, R), R), :],
@@ -96,9 +100,20 @@
                 device_id=(to, ch),
                 device_id_type=MESH,
             ).start()
-            return carry
-
-        lax.fori_loop(1, parts, one, 0)
+
+        z, x, core = me >> 3, (me >> 1) & 3, me & 1
+        for flip in range(2):
+            for steps in (STEPS[:8], STEPS[8:]):
+                code = sum((4 * dz + dx) << (4 * i) for i, (dz, dx) in enumerate(steps))
+                code = code - 2**32 if code >= 2**31 else code
+
+                def one(k, carry):
+                    step = (jnp.int32(code) >> (4 * k)) & 15
+                    send((((z + (step >> 2)) & 3) << 3) + (((x + step) & 3) << 1) + (core ^ flip))
+                    return carry
+
+                lax.fori_loop(0, len(steps), one, 0)
+        send(me ^ 1)
         own = pl.ds(pl.multiple_of(base + me * R, R), R)
         pltpu.make_async_copy(src.at[own, :], dst.at[own, :], recv_sem.at[kind, chunk]).start()
 
@@ -110,14 +125,21 @@
         sent = src.at[pl.ds(0, rows - R), :]
         pltpu.make_async_copy(sent, sent, send_sem.at[kind, chunk]).wait()
 
-    for chunk in range(chunks):
+    deal(0, 0, ht, hr)
+    for load in loads[chunks + 1 :]:
+        load.start()
+    for chunk in range(1, chunks):
+        loads[chunk].wait()
+        lax.fori_loop(chunk * rows // 128, (chunk + 1) * rows // 128, turn_filter, 0)
         deal(0, chunk, ht, hr)
 
+    loads[chunks + 1].wait()
     edge.wait_recv()
     first = jnp.where(me > 0, 1.0, 0.0).astype(F32)
 
     def short(m, at):
-        before = halo[m, :, at].astype(F32)[8:, :] * first
+        before = halo[:, at].astype(F32)[2 * m : 2 * m + 2, :] * first
+        before = jnp.concatenate([jnp.zeros((6, 128), F32), before], axis=0)
         ext = jnp.concatenate([before, qkv[m, :, at].astype(F32)], axis=0)
         return (
             sw_ref[m, 0:1, at] * ext[8:, :]
@@ -155,7 +177,7 @@
                 b[at * R : (at + 1) * R, :tok] = (re * cos + im * sin).astype(BF16)
                 b[at * R : (at + 1) * R, tok:] = (im * cos - re * sin).astype(BF16)
 
-    for load in loads[2:]:
+    for load in loads[chunks + 2 :]:
         load.wait()
 
     for chunk in range(chunks):
@@ -217,7 +239,7 @@
         hbm = pl.BlockSpec(memory_space=pl.ANY)
         return pl.pallas_call(
             functools.partial(kernel, parts),
-            out_shape=jax.ShapeDtypeStruct((tok, chans), BF16),
+            out_shape=pltpu.VMEM((tok, chans), BF16),
             in_specs=[hbm, vmem, hbm, vmem, hbm, hbm, hbm, hbm, vmem],
             out_specs=vmem,
             scratch_shapes=[
@@ -228,6 +250,8 @@
                 pltpu.VMEM(wi.shape, BF16),
                 pltpu.VMEM(g1.shape, BF16),
                 pltpu.VMEM((3, 16, chans), BF16),
+                pltpu.VMEM((16, chans), BF16),
+                pltpu.VMEM((16, chans), BF16),
                 pltpu.VMEM((chans, tok), BF16),
                 pltpu.VMEM((chans, tok), BF16),
                 pltpu.VMEM((chans, tok), BF16),
@@ -240,7 +264,7 @@
                 pltpu.VMEM((rows, 2 * tok), BF16),
                 pltpu.VMEM((rows, 2 * tok), BF16),
                 pltpu.VMEM((2 * rows, tok), BF16),
-                pltpu.SemaphoreType.DMA((6,)),
+                pltpu.SemaphoreType.DMA((chunks + 6,)),
                 pltpu.SemaphoreType.DMA((2,)),
                 pltpu.SemaphoreType.DMA((3, chunks)),
                 pltpu.SemaphoreType.DMA((3, chunks)),

time: 52.9 us -> 47.5 us (0.90); the launches traced: 52.2 us -> 47.4 us
  Pallas kernels: 49.9 us -> 46.4 us
  local copies, waits for them, and re-layouts: 2.26 us -> 0.97 us
    pallas_call x1, Pallas kernels: 49.9 us -> 46.4 us  [on_device(): pl.pallas_call(functools.partial(kernel, parts), out_shape=pltpu.VMEM((to...]
    unnamed x1, local copies, waits for them, and re-layouts: 2.26 us -> 0.97 us
where the time goes in v2:
time: 47.5 us; the launch traced here: 47.4 us
  Pallas kernels  46.4 us (98%)
  local copies, waits for them, and re-layouts  0.97 us (2%)
    pallas_call x1, Pallas kernels, on_device(): pl.pallas_call(functools.partial(kernel, parts), out_shape=pltpu.VMEM((to...  46.4 us
    unnamed x1, local copies, waits for them, and re-layouts  0.97 us

profile of v2, /device:TPU:1, one launch (start us, length us, event | category | flops | bytes accessed | tf_op | source)
XLA Modules:
  0.0 47.4 jit_solution(15989845596012930138)
XLA Ops:
  0.0 46.4 %shard_map.91 = bf16[512,1024]{1,0:T(8,128)(2,1)S(1)} custom-call(bf16[3,512,1024]{2,1,0:T(8,128)(2,1)} %qkv_hbm.1, f32[3,3,1024]{2,1,0:T(4,128)} %sw_ref.1, f32[512,1024]{1,0:T(8,128)} %filt_hbm.1, f32[1,1024]{1,0:T(1,128)} %bitcast.1, bf16[1024,512]{1,0:T(8,128)(2,1)} %constant.10.clone.f1_hbm, bf16[1024,1024]{1,0:T(8,128)(2,1)} %constant.11.clone.w_hbm, ...), custom_call_target="tpu_custom_call" | custom-call | tf_op jit(solution)/shard_map/pallas_call | solution.py:240
  46.4 1.0 %copy.11 = bf16[512,1024]{1,0:T(8,128)(2,1)} copy(bf16[512,1024]{1,0:T(8,128)(2,1)S(1)} %shard_map.91) | data formatting | bytes 2097152

commit v3 on v2

v3 whole, which is shorter than its diff:
```python
import functools

import jax
import jax.numpy as jnp
import numpy as np
from jax import lax
from jax.experimental import pallas as pl
from jax.experimental.pallas import tpu as pltpu
from jax.sharding import PartitionSpec as P

MESH = pl.DeviceIdType.MESH
C = 8
R = 16
STEPS = ((2, 2), (2, 1), (1, 2), (2, 3), (3, 2), (1, 1), (3, 3), (1, 3), (3, 1), (2, 0), (0, 2), (0, 1), (1, 0), (0, 3), (3, 0))
F32 = jnp.float32
BF16 = jnp.bfloat16


def dot(a, b):
    return jnp.dot(a, b, preferred_element_type=F32)


def tables(parts, tok):
    place = np.arange(parts)
    odd = 2 * place + 1
    angle = 2 * np.pi * np.outer(odd, place) / (4 * parts)
    spread = lambda m: np.kron(m, np.eye(R))
    f1 = np.concatenate([spread(np.cos(angle)), spread(-np.sin(angle))], axis=0)
    g1 = np.concatenate([spread(np.cos(angle).T), spread(-np.sin(angle).T)], axis=1)
    offset = np.arange(tok)
    angle = 2 * np.pi * (np.outer(offset, offset) % tok) / tok
    cos, sin = np.cos(angle), np.sin(angle)
    w = np.block([[cos, -sin], [sin, cos]])
    wi = np.block([[cos, sin], [-sin, cos]])
    angle = 2 * np.pi * np.outer(odd, offset) / (4 * parts * tok)
    tw = np.stack([np.cos(angle), np.sin(angle)])
    half = lambda m: m.astype(np.float32).astype(BF16)
    rest = lambda m: half(m - half(m).astype(np.float64))
    f1 = np.stack([half(f1), rest(f1)])
    g1 = np.stack([half(g1), rest(g1)])
    return f1, half(w), half(wi), g1, tw.astype(np.float32)


def kernel(
    parts, qkv_hbm, sw_hbm, filt_hbm, skip_hbm, f1_hbm, w_hbm, wi_hbm, g1_hbm, tw_hbm, o_ref,
    sw_ref, skip_ref, tw_ref, qkv, filt, f1, w, wi, g1, tail, ends, halo, ht, dt, hr, xr, ys, lt, drive, query, spec, b, y, g,
    load_sem, halo_sem, send_sem, recv_sem,
):
    me = lax.axis_index("seq")
    ch = lax.axis_index("ch")
    tok = qkv.shape[1]
    chans = qkv.shape[2]
    rows = parts * R
    lines = parts * C
    chunks = chans // lines
    half = tok // 2

    lanes = [pl.ds(chunk * lines, lines) for chunk in range(chunks)]
    loads = [
        pltpu.make_async_copy(src, dst, load_sem.at[i])
        for i, (src, dst) in enumerate(
            [(filt_hbm.at[:, at], filt.at[:, at]) for at in lanes]
            + [(qkv_hbm.at[:, pl.ds(tok - 16, 16), :], tail)]
            + [(qkv_hbm, qkv), (sw_hbm, sw_ref), (skip_hbm, skip_ref), (tw_hbm, tw_ref), (f1_hbm, f1), (w_hbm, w), (wi_hbm, wi), (g1_hbm, g1)]
        )
    ]
    for load in loads[: chunks + 1]:
        load.start()

    barrier = pltpu.get_barrier_semaphore()

    z, x, core = me >> 3, (me >> 1) & 3, me & 1

    def tour(steps, visit):
        for flip in range(2):
            for some in (steps[:8], steps[8:]):
                code = sum((4 * dz + dx) << (4 * i) for i, (dz, dx) in enumerate(some))
                code = code - 2**32 if code >= 2**31 else code

                def one(k, carry):
                    step = (jnp.int32(code) >> (4 * k)) & 15
                    visit((((z + (step >> 2)) & 3) << 3) + (((x + step) & 3) << 1) + (core ^ flip))
                    return carry

                lax.fori_loop(0, len(some), one, 0)
        visit(me ^ 1)

    def greet(to):
        pl.semaphore_signal(barrier, inc=1, device_id=(to, ch), device_id_type=MESH)

    tour(STEPS, greet)

    def turn(dst, j, value):
        value = value.T
        for d in range(128 // C):
            mine = value[d * C : (d + 1) * C, :]
            message = jnp.concatenate([mine[:, :half], mine[:, half:]], axis=0).astype(BF16)
            dst[pl.ds(pl.multiple_of(j * 128 * R // C + d * R, R), R), :] = message

    def turn_filter(j, carry):
        turn(ht, j, filt[:, pl.ds(pl.multiple_of(j * 128, 128), 128)])
        return carry

    loads[0].wait()
    lax.fori_loop(0, lines // 128, turn_filter, 0)
    loads[chunks].wait()
    last = [tail[m].astype(F32)[14:, :] for m in range(3)]
    ends[...] = jnp.concatenate(last + [jnp.zeros((10, chans), F32)], axis=0).astype(BF16)
    pl.semaphore_wait(barrier, parts - 1)

    edge = pltpu.make_async_remote_copy(
        src_ref=ends, dst_ref=halo, send_sem=halo_sem.at[0], recv_sem=halo_sem.at[1],
        device_id=((me + 1) & (parts - 1), ch), device_id_type=MESH,
    )
    edge.start()

    def deal(kind, chunk, src, dst):
        base = chunk * rows

        def send(to):
            pltpu.make_async_remote_copy(
                src_ref=src.at[pl.ds(pl.multiple_of(base + to * R, R), R), :],
                dst_ref=dst.at[pl.ds(pl.multiple_of(base + me * R, R), R), :],
                send_sem=send_sem.at[kind, chunk],
                recv_sem=recv_sem.at[kind, chunk],
                device_id=(to, ch),
                device_id_type=MESH,
            ).start()

        tour(STEPS, send)
        own = pl.ds(pl.multiple_of(base + me * R, R), R)
        pltpu.make_async_copy(src.at[own, :], dst.at[own, :], recv_sem.at[kind, chunk]).start()

    def arrived(kind, chunk, dst):
        whole = dst.at[pl.ds(pl.multiple_of(chunk * rows, rows), rows), :]
        pltpu.make_async_copy(whole, whole, recv_sem.at[kind, chunk]).wait()

    def left(kind, chunk, src):
        sent = src.at[pl.ds(0, rows - R), :]
        pltpu.make_async_copy(sent, sent, send_sem.at[kind, chunk]).wait()

    deal(0, 0, ht, hr)
    for load in loads[chunks + 1 :]:
        load.start()
    loads[chunks + 1].wait()
    loads[chunks + 2].wait()
    edge.wait_recv()
    first = jnp.where(me > 0, 1.0, 0.0).astype(F32)

    def short(m, at):
        before = halo[:, at].astype(F32)[2 * m : 2 * m + 2, :] * first
        before = jnp.concatenate([jnp.zeros((6, 128), F32), before], axis=0)
        ext = jnp.concatenate([before, qkv[m, :, at].astype(F32)], axis=0)
        return (
            sw_ref[m, 0:1, at] * ext[8:, :]
            + sw_ref[m, 1:2, at] * ext[7:-1, :]
            + sw_ref[m, 2:3, at] * ext[6:-2, :]
        )

    for chunk in range(chunks):

        def gate(j, carry):
            at = pl.ds(pl.multiple_of(j * 128, 128), 128)
            value = short(1, at) * short(2, at)
            drive[:, at] = value
            turn(dt, j, value)
            return carry

        if chunk:
            loads[chunk].wait()
            lax.fori_loop(chunk * lines // 128, (chunk + 1) * lines // 128, turn_filter, 0)
            deal(0, chunk, ht, hr)
        lax.fori_loop(chunk * lines // 128, (chunk + 1) * lines // 128, gate, 0)
        deal(1, chunk, dt, xr)

    def ask(j, carry):
        at = pl.ds(pl.multiple_of(j * 128, 128), 128)
        query[:, at] = short(0, at)
        return carry

    lax.fori_loop(0, chans // 128, ask, 0)

    def split(m_ref, at, value):
        return dot(m_ref[0, at, :], value) + dot(m_ref[1, at, :], value)

    def along_parts(blocks):
        real, imag = split(f1, slice(0, rows), blocks), split(f1, slice(rows, 2 * rows), blocks)
        for k in range(0, parts, 2):
            for n in range(2):
                at = slice(n * half, (n + 1) * half)
                turned = []
                for p in (k, k + 1):
                    cos, sin = tw_ref[0, p : p + 1, at], tw_ref[1, p : p + 1, at]
                    here = slice(p * R + n * C, p * R + (n + 1) * C)
                    re, im = real[here, :], imag[here, :]
                    turned.append((re * cos + im * sin, im * cos - re * sin))
                b[k * C : (k + 2) * C, n * half : (n + 1) * half] = jnp.concatenate(
                    [t[0] for t in turned], axis=0
                ).astype(BF16)
                b[k * C : (k + 2) * C, tok + n * half : tok + (n + 1) * half] = jnp.concatenate(
                    [t[1] for t in turned], axis=0
                ).astype(BF16)

    for load in loads[chunks + 3 :]:
        load.wait()

    def place(chunk):
        return pl.ds(pl.multiple_of(chunk * rows, rows), rows)

    def filter_spectra(chunk):
        arrived(0, chunk, hr)
        along_parts(hr[place(chunk), :])
        for n in range(4):
            spec[:, n * half : (n + 1) * half] = dot(b[...], w[:, n * half : (n + 1) * half])

    def convolve(chunk):
        arrived(1, chunk, xr)
        along_parts(xr[place(chunk), :])
        for n in range(2):
            real_at, imag_at = slice(n * half, (n + 1) * half), slice(tok + n * half, tok + (n + 1) * half)
            xre, xim = dot(b[...], w[:, real_at]), dot(b[...], w[:, imag_at])
            hre, him = spec[:, real_at], spec[:, imag_at]
            y[:, real_at] = (xre * hre - xim * him).astype(BF16)
            y[:, imag_at] = (xre * him + xim * hre).astype(BF16)
        back = [dot(y[...], wi[:, n * half : (n + 1) * half]) for n in range(4)]
        scale = 2.0 / (2 * parts * tok)
        for k in range(parts):
            turned = []
            for n in range(2):
                at = slice(n * half, (n + 1) * half)
                cos, sin = tw_ref[0, k : k + 1, at] * scale, tw_ref[1, k : k + 1, at] * scale
                re, im = back[n][k * C : (k + 1) * C, :], back[2 + n][k * C : (k + 1) * C, :]
                turned.append((re * cos - im * sin, im * cos + re * sin))
            for part in range(2):
                g[part * rows + k * R : part * rows + (k + 1) * R, :] = jnp.concatenate(
                    [t[part] for t in turned], axis=0
                ).astype(BF16)
        ys[place(chunk), :] = split(g1, slice(0, rows), g[...]).astype(BF16)

    def one_chunk(chunk, carry):
        filter_spectra(chunk)
        convolve(chunk)
        deal(2, chunk, ys, lt)
        return carry

    lax.fori_loop(0, chunks, one_chunk, 0)

    def finish(j, carry):
        at = pl.ds(pl.multiple_of(j * 128, 128), 128)
        came = lt[pl.ds(pl.multiple_of(j * 128 * R // C, 128 * R // C), 128 * R // C), :].astype(F32)
        for n in range(2):
            long_part = jnp.concatenate(
                [came[d * R + n * C : d * R + (n + 1) * C, :] for d in range(128 // C)], axis=0
            ).T
            here = slice(n * half, (n + 1) * half)
            o_ref[here, at] = (
                query[here, at] * (long_part + skip_ref[0:1, at] * drive[here, at])
            ).astype(BF16)
        return carry

    for chunk in range(chunks):
        arrived(2, chunk, lt)
        lax.fori_loop(chunk * lines // 128, (chunk + 1) * lines // 128, finish, 0)

    edge.wait_send()
    for chunk in range(chunks):
        left(0, chunk, ht)
        left(1, chunk, dt)
        left(2, chunk, ys)


def solution(mesh):
    parts = mesh.shape["seq"]

    def on_device(qkv, short_weight, long_filter, skip):
        tok, chans = long_filter.shape
        rows, lines = parts * R, parts * C
        chunks = chans // lines
        f1, w, wi, g1, tw = tables(parts, tok)
        vmem = pl.BlockSpec(memory_space=pltpu.VMEM)
        hbm = pl.BlockSpec(memory_space=pl.ANY)
        return pl.pallas_call(
            functools.partial(kernel, parts),
            out_shape=pltpu.VMEM((tok, chans), BF16),
            in_specs=[hbm] * 9,
            out_specs=vmem,
            scratch_shapes=[
                pltpu.VMEM(short_weight.shape, F32),
                pltpu.VMEM((1, chans), F32),
                pltpu.VMEM(tw.shape, F32),
                pltpu.VMEM(qkv.shape, BF16),
                pltpu.VMEM((tok, chans), F32),
                pltpu.VMEM(f1.shape, BF16),
                pltpu.VMEM(w.shape, BF16),
                pltpu.VMEM(wi.shape, BF16),
                pltpu.VMEM(g1.shape, BF16),
                pltpu.VMEM((3, 16, chans), BF16),
                pltpu.VMEM((16, chans), BF16),
                pltpu.VMEM((16, chans), BF16),
                pltpu.VMEM((chunks * rows, tok // 2), BF16),
                pltpu.VMEM((chunks * rows, tok // 2), BF16),
                pltpu.VMEM((chunks * rows, tok // 2), BF16),
                pltpu.VMEM((chunks * rows, tok // 2), BF16),
                pltpu.VMEM((chunks * rows, tok // 2), BF16),
                pltpu.VMEM((chunks * rows, tok // 2), BF16),
                pltpu.VMEM((tok, chans), F32),
                pltpu.VMEM((tok, chans), F32),
                pltpu.VMEM((lines, 2 * tok), F32),
                pltpu.VMEM((lines, 2 * tok), BF16),
                pltpu.VMEM((lines, 2 * tok), BF16),
                pltpu.VMEM((2 * rows, tok // 2), BF16),
                pltpu.SemaphoreType.DMA((chunks + 9,)),
                pltpu.SemaphoreType.DMA((2,)),
                pltpu.SemaphoreType.DMA((3, chunks)),
                pltpu.SemaphoreType.DMA((3, chunks)),
            ],
            compiler_params=pltpu.CompilerParams(
                collective_id=0, has_side_effects=True, vmem_limit_bytes=60 * 2**20
            ),
        )(qkv, short_weight, long_filter, skip[None, :], f1, w, wi, g1, tw)

    return jax.shard_map(
        on_device,
        mesh=mesh,
        in_specs=(P(None, "seq", "ch"), P(None, None, "ch"), P("seq", "ch"), P("ch")),
        out_specs=P("seq", "ch"),
        check_vma=False,
    )
```

time: 47.5 us -> 45.7 us (0.962)
  Pallas kernels: 46.4 us -> 44.6 us
    pallas_call x1, Pallas kernels: 46.4 us -> 44.6 us  [on_device(): pl.pallas_call(functools.partial(kernel, parts), out_shape=pltpu.VMEM((to...]
where the time goes in v3:
time: 45.7 us; the launch traced here: 45.5 us
  Pallas kernels  44.6 us (98%)
  local copies, waits for them, and re-layouts  0.97 us (2%)
    pallas_call x1, Pallas kernels, on_device(): pl.pallas_call(functools.partial(kernel, parts), out_shape=pltpu.VMEM((to...  44.6 us
    unnamed x1, local copies, waits for them, and re-layouts  0.97 us

profile of v3, /device:TPU:1, one launch (start us, length us, event | category | flops | bytes accessed | tf_op | source)
XLA Modules:
  0.0 45.5 jit_solution(1784185634457751095)
XLA Ops:
  0.0 44.6 %shard_map.91 = bf16[512,1024]{1,0:T(8,128)(2,1)S(1)} custom-call(bf16[3,512,1024]{2,1,0:T(8,128)(2,1)} %qkv_hbm.1, f32[3,3,1024]{2,1,0:T(4,128)} %sw_hbm.1, f32[512,1024]{1,0:T(8,128)} %filt_hbm.1, f32[1,1024]{1,0:T(1,128)} %bitcast.1, bf16[2,1024,512]{2,1,0:T(8,128)(2,1)} %constant.10.clone.f1_hbm, bf16[1024,1024]{1,0:T(8,128)(2,1)} %constant.11.clone.w_hbm, ...), custom_call_target="tpu_custom_call" | custom-call | tf_op jit(solution)/shard_map/pallas_call | solution.py:282
  44.6 1.0 %copy.11 = bf16[512,1024]{1,0:T(8,128)(2,1)} copy(bf16[512,1024]{1,0:T(8,128)(2,1)S(1)} %shard_map.91) | data formatting | bytes 2097152

commit v4 on v3

--- a/solution.py
+++ b/solution.py
@@ -64,14 +64,12 @@
             + [(qkv_hbm, qkv), (sw_hbm, sw_ref), (skip_hbm, skip_ref), (tw_hbm, tw_ref), (f1_hbm, f1), (w_hbm, w), (wi_hbm, wi), (g1_hbm, g1)]
         )
     ]
-    for load in loads[: chunks + 1]:
-        load.start()
 
     barrier = pltpu.get_barrier_semaphore()
 
     z, x, core = me >> 3, (me >> 1) & 3, me & 1
 
-    def tour(steps, visit):
+    def tour(steps, visit, side=None):
         for flip in range(2):
             for some in (steps[:8], steps[8:]):
                 code = sum((4 * dz + dx) << (4 * i) for i, (dz, dx) in enumerate(some))
@@ -79,7 +77,7 @@
 
                 def one(k, carry):
                     step = (jnp.int32(code) >> (4 * k)) & 15
-                    visit((((z + (step >> 2)) & 3) << 3) + (((x + step) & 3) << 1) + (core ^ flip))
+                    visit((((z + (step >> 2)) & 3) << 3) + (((x + step) & 3) << 1) + ((core ^ flip) if side is None else (side ^ flip)))
                     return carry
 
                 lax.fori_loop(0, len(some), one, 0)
@@ -89,6 +87,8 @@
         pl.semaphore_signal(barrier, inc=1, device_id=(to, ch), device_id_type=MESH)
 
     tour(STEPS, greet)
+    for load in loads[: chunks + 1]:
+        load.start()
 
     def turn(dst, j, value):
         value = value.T
@@ -127,7 +127,7 @@
                 device_id_type=MESH,
             ).start()
 
-        tour(STEPS, send)
+        tour(STEPS, send, 1 if kind == 2 else None)
         own = pl.ds(pl.multiple_of(base + me * R, R), R)
         pltpu.make_async_copy(src.at[own, :], dst.at[own, :], recv_sem.at[kind, chunk]).start()
 

time: 45.7 us -> 44.9 us (0.982)
  Pallas kernels: 44.6 us -> 43.8 us
    pallas_call x1, Pallas kernels: 44.6 us -> 43.8 us  [on_device(): pl.pallas_call(functools.partial(kernel, parts), out_shape=pltpu.VMEM((to...]
where the time goes in v4:
time: 44.9 us; the launch traced here: 44.8 us
  Pallas kernels  43.8 us (98%)
  local copies, waits for them, and re-layouts  0.97 us (2%)
    pallas_call x1, Pallas kernels, on_device(): pl.pallas_call(functools.partial(kernel, parts), out_shape=pltpu.VMEM((to...  43.8 us
    unnamed x1, local copies, waits for them, and re-layouts  0.97 us

profile of v4, /device:TPU:1, one launch (start us, length us, event | category | flops | bytes accessed | tf_op | source)
XLA Modules:
  0.0 44.8 jit_solution(13656187941515728718)
XLA Ops:
  0.0 43.8 %shard_map.91 = bf16[512,1024]{1,0:T(8,128)(2,1)S(1)} custom-call(bf16[3,512,1024]{2,1,0:T(8,128)(2,1)} %qkv_hbm.1, f32[3,3,1024]{2,1,0:T(4,128)} %sw_hbm.1, f32[512,1024]{1,0:T(8,128)} %filt_hbm.1, f32[1,1024]{1,0:T(1,128)} %bitcast.1, bf16[2,1024,512]{2,1,0:T(8,128)(2,1)} %constant.10.clone.f1_hbm, bf16[1024,1024]{1,0:T(8,128)(2,1)} %constant.11.clone.w_hbm, ...), custom_call_target="tpu_custom_call" | custom-call | tf_op jit(solution)/shard_map/pallas_call | solution.py:282
  43.8 1.0 %copy.11 = bf16[512,1024]{1,0:T(8,128)(2,1)} copy(bf16[512,1024]{1,0:T(8,128)(2,1)S(1)} %shard_map.91) | data formatting | bytes 2097152

commit v5 on v4

--- a/solution.py
+++ b/solution.py
@@ -38,7 +38,7 @@
     rest = lambda m: half(m - half(m).astype(np.float64))
     f1 = np.stack([half(f1), rest(f1)])
     g1 = np.stack([half(g1), rest(g1)])
-    return f1, half(w), half(wi), g1, tw.astype(np.float32)
+    return f1, np.stack([half(w), rest(w)]), half(wi), g1, tw.astype(np.float32)
 
 
 def kernel(
@@ -80,7 +80,7 @@
                     visit((((z + (step >> 2)) & 3) << 3) + (((x + step) & 3) << 1) + ((core ^ flip) if side is None else (side ^ flip)))
                     return carry
 
-                lax.fori_loop(0, len(some), one, 0)
+                lax.fori_loop(0, len(some), one, 0, unroll=True)
         visit(me ^ 1)
 
     def greet(to):
@@ -211,14 +211,14 @@
         arrived(0, chunk, hr)
         along_parts(hr[place(chunk), :])
         for n in range(4):
-            spec[:, n * half : (n + 1) * half] = dot(b[...], w[:, n * half : (n + 1) * half])
+            spec[:, n * half : (n + 1) * half] = dot(b[...], w[0, :, n * half : (n + 1) * half]) + dot(b[...], w[1, :, n * half : (n + 1) * half])
 
     def convolve(chunk):
         arrived(1, chunk, xr)
         along_parts(xr[place(chunk), :])
         for n in range(2):
             real_at, imag_at = slice(n * half, (n + 1) * half), slice(tok + n * half, tok + (n + 1) * half)
-            xre, xim = dot(b[...], w[:, real_at]), dot(b[...], w[:, imag_at])
+            xre, xim = dot(b[...], w[0, :, real_at]), dot(b[...], w[0, :, imag_at])
             hre, him = spec[:, real_at], spec[:, imag_at]
             y[:, real_at] = (xre * hre - xim * him).astype(BF16)
             y[:, imag_at] = (xre * him + xim * hre).astype(BF16)

time: 44.9 us -> 44.8 us (level)
  no operation moved by 1% of the time
where the time goes in v5:
time: 44.8 us; the launch traced here: 44.7 us
  Pallas kernels  43.7 us (98%)
  local copies, waits for them, and re-layouts  0.97 us (2%)
    pallas_call x1, Pallas kernels, on_device(): pl.pallas_call(functools.partial(kernel, parts), out_shape=pltpu.VMEM((to...  43.7 us
    unnamed x1, local copies, waits for them, and re-layouts  0.97 us

profile of v5, /device:TPU:1, one launch (start us, length us, event | category | flops | bytes accessed | tf_op | source)
XLA Modules:
  0.0 44.7 jit_solution(10754967713789193950)
XLA Ops:
  0.0 43.7 %shard_map.91 = bf16[512,1024]{1,0:T(8,128)(2,1)S(1)} custom-call(bf16[3,512,1024]{2,1,0:T(8,128)(2,1)} %qkv_hbm.1, f32[3,3,1024]{2,1,0:T(4,128)} %sw_hbm.1, f32[512,1024]{1,0:T(8,128)} %filt_hbm.1, f32[1,1024]{1,0:T(1,128)} %bitcast.1, bf16[2,1024,512]{2,1,0:T(8,128)(2,1)} %constant.10.clone.f1_hbm, bf16[2,1024,1024]{2,1,0:T(8,128)(2,1)} %constant.11.clone.w_hbm, ...), custom_call_target="tpu_custom_call" | custom-call | tf_op jit(solution)/shard_map/pallas_call | solution.py:282
  43.7 1.0 %copy.11 = bf16[512,1024]{1,0:T(8,128)(2,1)} copy(bf16[512,1024]{1,0:T(8,128)(2,1)S(1)} %shard_map.91) | data formatting | bytes 2097152

commit v6 on v5

--- a/solution.py
+++ b/solution.py
@@ -43,7 +43,7 @@
 
 def kernel(
     parts, qkv_hbm, sw_hbm, filt_hbm, skip_hbm, f1_hbm, w_hbm, wi_hbm, g1_hbm, tw_hbm, o_ref,
-    sw_ref, skip_ref, tw_ref, qkv, filt, f1, w, wi, g1, tail, ends, halo, ht, dt, hr, xr, ys, lt, drive, query, spec, b, y, g,
+    sw_ref, skip_ref, tw_ref, qkv, filt, f1, w, wi, g1, tail, ends, halo, before, ht, dt, hr, xr, ys, lt, drive, query, spec, b, y, g,
     load_sem, halo_sem, send_sem, recv_sem,
 ):
     me = lax.axis_index("seq")
@@ -102,10 +102,11 @@
         return carry
 
     loads[0].wait()
-    lax.fori_loop(0, lines // 128, turn_filter, 0)
+    lax.fori_loop(0, lines // 128, turn_filter, 0, unroll=True)
     loads[chunks].wait()
     last = [tail[m].astype(F32)[14:, :] for m in range(3)]
-    ends[...] = jnp.concatenate(last + [jnp.zeros((10, chans), F32)], axis=0).astype(BF16)
+    last = [row[:, at : at + chans // 2] for row in last for at in (0, chans // 2)]
+    ends[...] = jnp.concatenate(last + [jnp.zeros((4, chans // 2), F32)], axis=0).astype(BF16)
     pl.semaphore_wait(barrier, parts - 1)
 
     edge = pltpu.make_async_remote_copy(
@@ -145,12 +146,15 @@
     loads[chunks + 1].wait()
     loads[chunks + 2].wait()
     edge.wait_recv()
-    first = jnp.where(me > 0, 1.0, 0.0).astype(F32)
+    ended = halo[...].astype(F32)
+    for m in range(3):
+        both = [ended[4 * m + 2 * n : 4 * m + 2 * n + 2, :] for n in range(2)]
+        both = jnp.concatenate([jnp.concatenate(both, axis=1), jnp.zeros((6, chans), F32)], axis=0)
+        before[m] = both * jnp.where(me > 0, 1.0, 0.0).astype(F32)
 
     def short(m, at):
-        before = halo[:, at].astype(F32)[2 * m : 2 * m + 2, :] * first
-        before = jnp.concatenate([jnp.zeros((6, 128), F32), before], axis=0)
-        ext = jnp.concatenate([before, qkv[m, :, at].astype(F32)], axis=0)
+        above = jnp.concatenate([jnp.zeros((6, 128), F32), before[m, :2, at]], axis=0)
+        ext = jnp.concatenate([above, qkv[m, :, at].astype(F32)], axis=0)
         return (
             sw_ref[m, 0:1, at] * ext[8:, :]
             + sw_ref[m, 1:2, at] * ext[7:-1, :]
@@ -168,9 +172,9 @@
 
         if chunk:
             loads[chunk].wait()
-            lax.fori_loop(chunk * lines // 128, (chunk + 1) * lines // 128, turn_filter, 0)
+            lax.fori_loop(chunk * lines // 128, (chunk + 1) * lines // 128, turn_filter, 0, unroll=True)
             deal(0, chunk, ht, hr)
-        lax.fori_loop(chunk * lines // 128, (chunk + 1) * lines // 128, gate, 0)
+        lax.fori_loop(chunk * lines // 128, (chunk + 1) * lines // 128, gate, 0, unroll=True)
         deal(1, chunk, dt, xr)
 
     def ask(j, carry):
@@ -260,7 +264,7 @@
 
     for chunk in range(chunks):
         arrived(2, chunk, lt)
-        lax.fori_loop(chunk * lines // 128, (chunk + 1) * lines // 128, finish, 0)
+        lax.fori_loop(chunk * lines // 128, (chunk + 1) * lines // 128, finish, 0, unroll=True)
 
     edge.wait_send()
     for chunk in range(chunks):
@@ -295,8 +299,9 @@
                 pltpu.VMEM(wi.shape, BF16),
                 pltpu.VMEM(g1.shape, BF16),
                 pltpu.VMEM((3, 16, chans), BF16),
-                pltpu.VMEM((16, chans), BF16),
-                pltpu.VMEM((16, chans), BF16),
+                pltpu.VMEM((16, chans // 2), BF16),
+                pltpu.VMEM((16, chans // 2), BF16),
+                pltpu.VMEM((3, 8, chans), F32),
                 pltpu.VMEM((chunks * rows, tok // 2), BF16),
                 pltpu.VMEM((chunks * rows, tok // 2), BF16),
                 pltpu.VMEM((chunks * rows, tok // 2), BF16),

time: 44.8 us -> 44.5 us (level)
  no operation moved by 1% of the time
where the time goes in v6:
time: 44.5 us; the launch traced here: 44.4 us
  Pallas kernels  43.4 us (98%)
  local copies, waits for them, and re-layouts  0.97 us (2%)
    pallas_call x1, Pallas kernels, on_device(): pl.pallas_call(functools.partial(kernel, parts), out_shape=pltpu.VMEM((to...  43.4 us
    unnamed x1, local copies, waits for them, and re-layouts  0.97 us

profile of v6, /device:TPU:1, one launch (start us, length us, event | category | flops | bytes accessed | tf_op | source)
XLA Modules:
  0.0 44.4 jit_solution(2625658390087519235)
XLA Ops:
  0.0 43.4 %shard_map.91 = bf16[512,1024]{1,0:T(8,128)(2,1)S(1)} custom-call(bf16[3,512,1024]{2,1,0:T(8,128)(2,1)} %qkv_hbm.1, f32[3,3,1024]{2,1,0:T(4,128)} %sw_hbm.1, f32[512,1024]{1,0:T(8,128)} %filt_hbm.1, f32[1,1024]{1,0:T(1,128)} %bitcast.1, bf16[2,1024,512]{2,1,0:T(8,128)(2,1)} %constant.10.clone.f1_hbm, bf16[2,1024,1024]{2,1,0:T(8,128)(2,1)} %constant.11.clone.w_hbm, ...), custom_call_target="tpu_custom_call" | custom-call | tf_op jit(solution)/shard_map/pallas_call | solution.py:286
  43.4 1.0 %copy.11 = bf16[512,1024]{1,0:T(8,128)(2,1)} copy(bf16[512,1024]{1,0:T(8,128)(2,1)S(1)} %shard_map.91) | data formatting | bytes 2097152

commit v7 on v5

--- a/solution.py
+++ b/solution.py
@@ -173,9 +173,13 @@
         lax.fori_loop(chunk * lines // 128, (chunk + 1) * lines // 128, gate, 0)
         deal(1, chunk, dt, xr)
 
+    loads[chunks + 3].wait()
+
     def ask(j, carry):
         at = pl.ds(pl.multiple_of(j * 128, 128), 128)
-        query[:, at] = short(0, at)
+        asked = short(0, at)
+        query[:, at] = asked
+        drive[:, at] = asked * (skip_ref[0:1, at] * drive[:, at])
         return carry
 
     lax.fori_loop(0, chans // 128, ask, 0)
@@ -201,7 +205,7 @@
                     [t[1] for t in turned], axis=0
                 ).astype(BF16)
 
-    for load in loads[chunks + 3 :]:
+    for load in loads[chunks + 4 :]:
         load.wait()
 
     def place(chunk):
@@ -254,7 +258,7 @@
             ).T
             here = slice(n * half, (n + 1) * half)
             o_ref[here, at] = (
-                query[here, at] * (long_part + skip_ref[0:1, at] * drive[here, at])
+                query[here, at] * long_part + drive[here, at]
             ).astype(BF16)
         return carry
 

time: 44.8 us -> 45.1 us (level)
  no operation moved by 1% of the time
where the time goes in v7:
time: 45.1 us; the launch traced here: 44.9 us
  Pallas kernels  44 us (98%)
  local copies, waits for them, and re-layouts  0.97 us (2%)
    pallas_call x1, Pallas kernels, on_device(): pl.pallas_call(functools.partial(kernel, parts), out_shape=pltpu.VMEM((to...  44 us
    unnamed x1, local copies, waits for them, and re-layouts  0.97 us

profile of v7, /device:TPU:1, one launch (start us, length us, event | category | flops | bytes accessed | tf_op | source)
XLA Modules:
  0.0 44.9 jit_solution(18171399969449929531)
XLA Ops:
  0.0 44.0 %shard_map.91 = bf16[512,1024]{1,0:T(8,128)(2,1)S(1)} custom-call(bf16[3,512,1024]{2,1,0:T(8,128)(2,1)} %qkv_hbm.1, f32[3,3,1024]{2,1,0:T(4,128)} %sw_hbm.1, f32[512,1024]{1,0:T(8,128)} %filt_hbm.1, f32[1,1024]{1,0:T(1,128)} %bitcast.1, bf16[2,1024,512]{2,1,0:T(8,128)(2,1)} %constant.10.clone.f1_hbm, bf16[2,1024,1024]{2,1,0:T(8,128)(2,1)} %constant.11.clone.w_hbm, ...), custom_call_target="tpu_custom_call" | custom-call | tf_op jit(solution)/shard_map/pallas_call | solution.py:286
  44.0 1.0 %copy.11 = bf16[512,1024]{1,0:T(8,128)(2,1)} copy(bf16[512,1024]{1,0:T(8,128)(2,1)S(1)} %shard_map.91) | data formatting | bytes 2097152
